TPU v7x, 32 devices: a whole 2x2x4 slice. The times are simulated.
32 devices in a mesh: rows: 32 (over z, y, x, core).
Axes of the slice: x: 2, y: 2, z: 4, core: 2. Of those that a mesh axis runs over, the one named last changes fastest.
Arguments:
- sketch: float32 [65536, 512], P('rows'), may hold values from -100 to 100
- panel: float32 [65536, 512], P('rows'), may hold values from -6 to 6
Outputs:
- basis: float32 [65536, 512], P('rows')
- projected: float32 [512, 512], P('rows')
All inputs are finite; a program needn't handle non-finite values.
Results may differ from a plain program's by a relative error of at most 0.00029.
Values sent between devices are 32-bit elements; how exact they have to be, the bound alone decides.
A program may use at most 64 MiB of HBM per device.

v0:
```python
import jax
import jax.numpy as jnp
from jax import lax
from jax.sharding import PartitionSpec as P


def on_device(sketch, panel):
    highest = lax.Precision.HIGHEST
    count = lax.axis_size("rows")
    total_rows = sketch.shape[0] * count
    local_gram = (
        lax.dot_general(
            sketch,
            sketch,
            (((0,), (0,)), ((), ())),
            precision=highest,
            preferred_element_type=jnp.float32,
        )
        / total_rows
    )
    scale = 1.0 / jnp.sqrt(jnp.float32(total_rows))
    raw_share = lax.psum_scatter(
        lax.dot_general(
            panel,
            sketch,
            (((0,), (0,)), ((), ())),
            precision=highest,
            preferred_element_type=jnp.float32,
        ),
        "rows",
        scatter_dimension=0,
        tiled=True,
    )
    gram = lax.psum(local_gram, "rows")
    lower = jnp.linalg.cholesky(gram)
    basis = jax.scipy.linalg.solve_triangular(lower, sketch.T, lower=True).T
    projected = jax.scipy.linalg.solve_triangular(lower, raw_share.T, lower=True).T * scale
    return (basis, projected)


def solution(mesh):
    return jax.shard_map(
        on_device,
        mesh=mesh,
        in_specs=(P("rows", None), P("rows", None)),
        out_specs=(P("rows", None), P("rows", None)),
        check_vma=False,
    )
```

profile of v0, /device:TPU:0, one launch (start us, length us, event | category | flops | bytes accessed | tf_op | source)
XLA Modules:
  0.0 323.4 jit_solution(7146548030011768634)
XLA Ops:
  7.2 11.2 %convolution_multiply_fusion = f32[512,512]{0,1:T(8,128)} fusion(f32[2048,512]{1,0:T(8,128)} %param.2), kind=kOutput, calls=%fused_computation.15 | convolution fusion | flops 6442713088 | bytes 5242880 | tf_op jit(solution)/shard_map/dot_general | solution.py:12
  18.5 10.3 %fusion.54 = f32[512,512]{1,0:T(8,128)} fusion(f32[2048,512]{1,0:T(8,128)} %param.3, f32[2048,512]{1,0:T(8,128)} %param.2), kind=kOutput, calls=%fused_computation.92 | convolution fusion | flops 6442450944 | bytes 9437184 | tf_op jit(solution)/shard_map/dot_general | solution.py:23
  28.9 122.3 %all-reduce.3.cloned.1.call-done = f32[512,512]{0,1:T(8,128)} async-done(((f32[512,512]{0,1:T(8,128)}), f32[512,512]{0,1:T(8,128)}) %all-reduce.3.cloned.1.call-update) | async-done | bytes 1048592 | tf_op jit(solution)/shard_map/psum | solution.py:34
  151.2 1.6 copy.5
  152.8 1.4 fusion.14
  154.3 11.7 %cholesky.104 = f32[128,128]{1,0:T(8,128)S(1)} custom-call(f32[128,128]{1,0:T(8,128)S(1)} %cholesky.266), custom_call_target="Cholesky" | custom-call | tf_op jit(solution)/shard_map/jit(cholesky)/cholesky | solution.py:35
  166.0 9.8 %custom-call.34 = f32[1,128,128]{1,2,0:T(8,128)S(1)} custom-call(f32[1,128,128]{2,1,0:T(8,128)S(1)} %get-tuple-element.31), custom_call_target="InvertDiagBlocksLowerTriangular" | custom-call | tf_op jit(solution)/shard_map/jit(cholesky)/cholesky | solution.py:35
  176.6 11.7 %cholesky.217 = f32[128,128]{1,0:T(8,128)S(1)} custom-call(f32[128,128]{1,0:T(8,128)S(1)} %cholesky.270), custom_call_target="Cholesky" | custom-call | tf_op jit(solution)/shard_map/jit(cholesky)/cholesky | solution.py:35
  188.4 10.2 %custom-call.35 = f32[1,128,128]{1,2,0:T(8,128)S(1)} custom-call(f32[1,128,128]{2,1,0:T(8,128)S(1)} %get-tuple-element.28), custom_call_target="InvertDiagBlocksLowerTriangular" | custom-call | tf_op jit(solution)/shard_map/jit(cholesky)/cholesky | solution.py:35
  199.2 11.7 %cholesky.238 = f32[128,128]{1,0:T(8,128)S(1)} custom-call(f32[128,128]{1,0:T(8,128)S(1)} %cholesky.275), custom_call_target="Cholesky" | custom-call | tf_op jit(solution)/shard_map/jit(cholesky)/cholesky | solution.py:35
  211.0 0.7 compare_reduce_fusion.1
  211.7 9.8 %custom-call.36 = f32[1,128,128]{1,2,0:T(8,128)S(1)} custom-call(f32[1,128,128]{2,1,0:T(8,128)S(1)} %get-tuple-element.25), custom_call_target="InvertDiagBlocksLowerTriangular" | custom-call | tf_op jit(solution)/shard_map/jit(cholesky)/cholesky | solution.py:35
  222.1 11.7 %cholesky.255 = f32[128,128]{1,0:T(8,128)S(1)} custom-call(f32[128,128]{1,0:T(8,128)S(1)} %convolution_subtract_fusion.4), custom_call_target="Cholesky" | custom-call | tf_op jit(solution)/shard_map/jit(cholesky)/cholesky | solution.py:35
  238.0 8.5 %while.1 = (s32[]{:T(128)}, f32[512,512]{1,0:T(8,128)S(1)}, s32[4,2]{0,1:T(2,128)S(1)}, f32[4,128,128]{2,1,0:T(8,128)S(1)}, s32[]{:T(128)}) while((s32[]{:T(128)}, f32[512,512]{1,0:T(8,128)S(1)}, s32[4,2]{0,1:T(2,128)S(1)}, f32[4,128,128]{2,1,0:T(8,128)S(1)}, s32[]{:T(128)}) %tuple.32), condition=%wide.while_cond, body=%wide.while_body.sunk | while | flops 2 | bytes 131189 | solution.py:36
  238.7 1.4 bitcast_dynamic-update-slice_fusion.2
  240.8 1.4 bitcast_dynamic-update-slice_fusion.2
  243.0 1.4 bitcast_dynamic-update-slice_fusion.2
  245.1 1.4 bitcast_dynamic-update-slice_fusion.2
  246.5 39.3 %custom-call.37 = f32[4,128,128]{1,2,0:T(8,128)S(1)} custom-call(f32[4,128,128]{2,1,0:T(8,128)S(1)} %get-tuple-element.9), custom_call_target="InvertDiagBlocksLowerTriangular" | custom-call | tf_op jit(solution)/shard_map/jit(_solve_triangular)/triangular_solve | solution.py:36
  285.9 2.4 fusion.12
  288.3 3.0 convolution_subtract_fusion.1
  291.3 1.1 fusion.32
  292.4 3.5 %convolution_subtract_fusion = f32[128,2048]{0,1:T(8,128)S(1)} fusion(f32[128,2048]{1,0:T(8,128)S(1)} %fusion.32, f32[128,2048]{1,0:T(8,128)S(1)} %fusion.12, f32[512,2048]{0,1:T(8,128)S(1)} %bitcast.68, f32[512,512]{1,0:T(8,128)S(1)} %get-tuple-element.82), kind=kOutput, calls=%fused_computation.10 | convolution fusion | flops 806092800 | bytes 4325376 | tf_op jit(solution)/shard_map/jit(_solve_triangular)/triangular_solve | solution.py:36
  296.0 1.1 fusion.34
  297.1 5.6 %fusion.6 = f32[128,2048]{0,1:T(8,128)S(1)} fusion(f32[128,2048]{1,0:T(8,128)S(1)} %fusion.34, f32[128,2048]{1,0:T(8,128)S(1)} %fusion.32, f32[128,2048]{1,0:T(8,128)S(1)} %fusion.12, f32[512,2048]{0,1:T(8,128)S(1)} %bitcast.69, f32[512,512]{1,0:T(8,128)S(1)} %get-tuple-element.82), kind=kOutput, calls=%fused_computation.9 | convolution fusion | flops 1209794560 | bytes 5439488 | tf_op jit(solution)/shard_map/jit(_solve_triangular)/triangular_solve | solution.py:36
  302.6 1.1 fusion.36
  303.7 2.4 maximum_bitcast_fusion
  306.1 5.3 %copy.6 = f32[2048,512]{1,0:T(8,128)} copy(f32[2048,512]{0,1:T(8,128)} %maximum_bitcast_fusion) | data formatting | bytes 8388608
  311.5 0.9 fusion.30
  312.3 0.9 convolution_subtract_fusion.7
  313.4 0.9 convolution_subtract_fusion.6
  314.5 1.0 convolution_subtract_fusion.5
  (39 shorter events, 7.8 us)
Async XLA Ops:
  7.2 144.1 %all-reduce.3.cloned.1.call-start = ((), (), s32[]{:S(2)}) async-start(), calls=%async_computation.1 | async-start | bytes 2097152 | tf_op jit(solution)/shard_map/psum | solution.py:34
  18.5 293.0 %reduce-scatter.2.cloned.1.call-start = ((), (), s32[]{:S(2)}) async-start(), calls=%async_computation.2 | async-start | bytes 1081344 | tf_op jit(solution)/shard_map/reduce_scatter | solution.py:22
  285.8 6.6 %copy-start = (f32[2048,512]{1,0:T(8,128)S(1)}, f32[2048,512]{1,0:T(8,128)}, u32[]{:S(2)}) copy-start(f32[2048,512]{1,0:T(8,128)} %param.2) | copy-start | bytes 12582916
Sparse Core Ops, SparseCore 0:
  18.6 132.5 all-reduce.2
  153.6 134.6 reduce-scatter.1
where the time goes:
time: 330 us; the launch traced here: 323 us
  other arithmetic  123 us (37%)
  waiting for transfers between devices  122 us (37%)
  matrix products  45.5 us (14%)
  between operations  17 us (5%)
  local copies, waits for them, and re-layouts  15.4 us (5%)
    psum x1, waiting for transfers between devices, on_device(): gram = lax.psum(local_gram, 'rows')  122 us
    another operation x14, other arithmetic, on_device(): lower = jnp.linalg.cholesky(gram)  78.8 us
    another operation x3, other arithmetic, on_device(): basis = jax.scipy.linalg.solve_triangular(lower, sketch.T, lower=True).T  39.6 us
    another operation x7, matrix products, on_device(): basis = jax.scipy.linalg.solve_triangular(lower, sketch.T, lower=True).T  17.8 us
    dot_general x1, matrix products, on_device(): lax.dot_general(sketch, sketch, (((0,), (0,)), ((), ())), precision=highe...  11.2 us
    dot_general x1, matrix products, on_device(): lax.dot_general(panel, sketch, (((0,), (0,)), ((), ())), precision=highes...  10.3 us
    another operation x12, local copies, waits for them, and re-layouts  8.39 us
  transfers between devices with their start and end apart: 2, of which 1 were waited for; matrix products, arithmetic and copies ran while one was open for 52% of the time, Pallas kernels for 0%

commit v1 on v0

v1 whole, which is shorter than its diff:
```python
import functools
import jax
import jax.numpy as jnp
from jax import lax
from jax.experimental import pallas as pl
from jax.experimental.pallas import tpu as pltpu
from jax.sharding import PartitionSpec as P

HI = lax.Precision.HIGHEST
BLK = 128
SUB = 8


def splat(x, i, j):
    return jnp.broadcast_to(x[i : i + 1, j : j + 1], (SUB, BLK))


def row(x, i):
    return jnp.broadcast_to(x[i : i + 1, :], (SUB, BLK))


def lane(x, j):
    return jnp.broadcast_to(x[:, j : j + 1], (SUB, BLK))


def small_inverse(a):
    n = SUB
    a = [list(r) for r in a]
    t = [[None] * n for _ in range(n)]
    for k in range(n):
        r = lax.rsqrt(a[k][k])
        l = {i: a[i][k] * r for i in range(k + 1, n)}
        for j in range(k + 1, n):
            for i in range(j, n):
                a[i][j] = a[i][j] - l[i] * l[j]
        t[k][k] = r
        for m in range(k):
            t[k][m] = t[k][m] * r
        for i in range(k + 1, n):
            for m in range(k + 1):
                e = l[i] * t[k][m]
                t[i][m] = -e if t[i][m] is None else t[i][m] - e
    return t


def block_inverse(a_ref, out_ref, base):
    lanes = lax.broadcasted_iota(jnp.int32, (SUB, BLK), 1)
    subs = lax.broadcasted_iota(jnp.int32, (SUB, BLK), 0)
    steps = BLK // SUB
    strips = [a_ref[i * SUB : (i + 1) * SUB, :] for i in range(steps)]
    for j in range(steps):
        j0 = j * SUB
        cur = strips[j]
        cols = [lane(cur, j0 + m) for m in range(SUB)]
        a = [[row(cols[m], i) for m in range(i + 1)] for i in range(SUB)]
        t = small_inverse(a)
        here = (lanes >= j0) & (lanes < j0 + SUB)
        mixed = jnp.where(here, jnp.where(lanes - j0 == subs, 1.0, 0.0), cur)
        rows = [row(mixed, m) for m in range(SUB)]
        r = []
        for k in range(SUB):
            acc = t[k][0] * rows[0]
            for m in range(1, k + 1):
                acc = acc + t[k][m] * rows[m]
            r.append(acc)
        if j + 1 < steps:
            q = []
            for k in range(SUB):
                acc = t[k][k] * r[k]
                for m in range(k + 1, SUB):
                    acc = acc + t[m][k] * r[m]
                q.append(acc)
            for i in range(j + 1, steps):
                x = strips[i]
                new = jnp.where(here, 0.0, x)
                for m in range(SUB):
                    new = new - lane(x, j0 + m) * q[m]
                strips[i] = new
        res = r[0]
        for k in range(1, SUB):
            res = jnp.where(subs == k, r[k], res)
        out_ref[j0 : j0 + SUB, :] = jnp.where(lanes <= j0 + subs, res, 0.0)


def inverse_factor(work, diag, dinv):
    n = work.shape[0]
    blocks = n // BLK
    ids = lax.broadcasted_iota(jnp.int32, (BLK, n), 1)
    subs = lax.broadcasted_iota(jnp.int32, (BLK, n), 0)

    def outer(p, c):
        at = pl.multiple_of(p * BLK, BLK)
        diag[...] = work[pl.ds(at, BLK), pl.ds(at, BLK)]
        block_inverse(diag, dinv, 0)
        work[pl.ds(at, BLK), pl.ds(at, BLK)] = jnp.where(
            lax.broadcasted_iota(jnp.int32, (BLK, BLK), 0) == lax.broadcasted_iota(jnp.int32, (BLK, BLK), 1), 1.0, 0.0)
        r = jnp.dot(dinv[...], work[pl.ds(at, BLK), :], precision=HI, preferred_element_type=jnp.float32)
        work[pl.ds(at, BLK), :] = r

        def update(q, c):
            to = pl.multiple_of(q * BLK, BLK)
            u = work[pl.ds(at, BLK), pl.ds(to, BLK)]
            work[pl.ds(to, BLK), pl.ds(at, BLK)] = jnp.zeros((BLK, BLK), jnp.float32)
            work[pl.ds(to, BLK), :] -= lax.dot_general(u, work[pl.ds(at, BLK), :], (((0,), (0,)), ((), ())), precision=HI, preferred_element_type=jnp.float32)
            return c

        lax.fori_loop(p + 1, blocks, update, 0)
        return c

    lax.fori_loop(0, blocks, outer, 0)


def split(x):
    hi = x.astype(jnp.bfloat16)
    return hi, (x - hi.astype(jnp.float32)).astype(jnp.bfloat16)


def over_rows(a, b):
    return lax.dot_general(a, b, (((0,), (0,)), ((), ())), preferred_element_type=jnp.float32)


def pairs(n):
    blocks = n // BLK
    return [(p, q) for p in range(blocks) for q in range(p, blocks)]


def sums_kernel(
    radices, s_hbm, p_hbm, full, share,
    s_buf, p_buf, gacc, g, g1, g2, g3, r, r1, r2, r3, in_sem,
    send_g, recv_g, send_r, recv_r, send_a, recv_a,
):
    ra, rb, rc = radices
    count = ra * rb * rc
    me = lax.axis_index("rows")
    a, b, c = lax.rem(me, ra), lax.rem(me // ra, rb), me // (ra * rb)
    k = s_buf.shape[1]
    rows = s_buf.shape[0]
    parts = in_sem.shape[1]
    step = rows // parts

    def load(t, i):
        src, dst = ((s_hbm, s_buf), (p_hbm, p_buf))[t]
        at = pl.ds(i * step, step)
        return pltpu.make_async_copy(src.at[at], dst.at[at], in_sem.at[t, i])

    for t in range(2):
        for i in range(parts):
            load(t, i).start()

    def device(x, y, z):
        return (x + ra * (y + rb * z),)

    def partner(stage, o):
        if stage == 0:
            d = lax.rem(a + o, ra)
            return device(d, b, c), d
        if stage == 1:
            d = lax.rem(b + o, rb)
            return device(a, d, c), d
        d = lax.rem(c + o, rc)
        return device(a, b, d), d

    barrier = pltpu.get_barrier_semaphore()
    for stage in range(3):
        for o in range(1, radices[stage]):
            pl.semaphore_signal(barrier, inc=1, device_id=partner(stage, o)[0], device_id_type=pl.DeviceIdType.MESH)

    digits = (a, b, c)

    def base_of(unit, stage):
        if stage == 0:
            return 0
        if stage == 1:
            return a * (rb * rc * unit)
        if stage == 2:
            return a * (rb * rc * unit) + b * (rc * unit)
        return a * (rb * rc * unit) + b * (rc * unit) + c * unit

    def width(unit, stage):
        return unit * (rb * rc, rc, 1)[stage]

    def reduce_copy(buf, recv, ss, rs, unit, stage, o, incoming):
        dev, d = partner(stage, o)
        w = width(unit, stage)
        at = pl.multiple_of(base_of(unit, stage) + d * w, 8)
        slot = d if incoming else digits[stage]
        return pltpu.make_async_remote_copy(
            src_ref=buf.at[pl.ds(at, w)], dst_ref=recv[stage].at[slot],
            send_sem=ss.at[stage, o], recv_sem=rs.at[stage, slot],
            device_id=dev, device_id_type=pl.DeviceIdType.MESH)

    def reduce_start(buf, recv, ss, rs, unit, stage):
        for o in range(1, radices[stage]):
            reduce_copy(buf, recv, ss, rs, unit, stage, o, False).start()

    def reduce_end(buf, recv, ss, rs, unit, stage, out=None):
        w = width(unit, stage)
        at = pl.ds(pl.multiple_of(base_of(unit, stage + 1), 8), w)
        total = buf[at, :]
        for o in range(1, radices[stage]):
            reduce_copy(buf, recv, ss, rs, unit, stage, o, True).wait_recv()
            total = total + recv[stage][partner(stage, o)[1]]
        if out is None:
            buf[at, :] = total
        else:
            out(total)
        for o in range(1, radices[stage]):
            reduce_copy(buf, recv, ss, rs, unit, stage, o, False).wait_send()

    def gather_copy(buf, ss, rs, unit, stage, o, incoming):
        dev, d = partner(stage, o)
        w = width(unit, stage)
        digit = d if incoming else digits[stage]
        at = pl.multiple_of(base_of(unit, stage) + digit * w, 8)
        return pltpu.make_async_remote_copy(
            src_ref=buf.at[pl.ds(at, w)], dst_ref=buf.at[pl.ds(at, w)],
            send_sem=ss.at[stage, o], recv_sem=rs.at[stage, digit],
            device_id=dev, device_id_type=pl.DeviceIdType.MESH)

    for i in range(parts):
        load(0, i).wait()
        hi, lo = split(s_buf[i * step : (i + 1) * step, :])
        both = over_rows(hi, jnp.concatenate([hi, lo], axis=1))
        if i == 0:
            gacc[...] = both
        else:
            gacc[...] += both
    inv = 1.0 / (rows * count)
    for n, (p, q) in enumerate(pairs(k)):
        rp, rq = slice(p * BLK, (p + 1) * BLK), slice(q * BLK, (q + 1) * BLK)
        mid = gacc[rp, k + q * BLK : k + (q + 1) * BLK]
        mir = gacc[rq, k + p * BLK : k + (p + 1) * BLK]
        g[n * BLK : (n + 1) * BLK, :] = (gacc[rp, rq] + (mid + mir.T)) * inv
    ug = g.shape[0] // count
    gr = (g, (g1, g2, g3), send_g, recv_g, ug)
    pl.semaphore_wait(barrier, ra + rb + rc - 3)
    reduce_start(*gr, 0)

    fr = p_buf.shape[1] // count
    for i in range(parts):
        load(1, i).wait()

    def product(f0):
        acc = None
        for i in range(parts):
            at = slice(i * step, (i + 1) * step)
            hi, lo = split(s_buf[at, :])
            ph, plo = split(p_buf[at, f0 : f0 + BLK])
            both = over_rows(ph, jnp.concatenate([hi, lo], axis=1))
            t = both[:, :k] + (both[:, k:] + over_rows(plo, hi))
            acc = t if acc is None else acc + t
        for m in range(BLK // fr):
            d = f0 // fr + m
            pos = (d % ra) * (rb * rc) + ((d // ra) % rb) * rc + d // (ra * rb)
            r[pos * fr : (pos + 1) * fr, :] = acc[m * fr : (m + 1) * fr, :]

    todo = list(range(0, p_buf.shape[1], BLK))
    product(todo[0])
    reduce_end(*gr, 0)
    reduce_start(*gr, 1)
    for f0 in todo[1:]:
        product(f0)
    reduce_end(*gr, 1)
    reduce_start(*gr, 2)
    rr = (r, (r1, r2, r3), send_r, recv_r, fr)
    reduce_start(*rr, 0)

    def put(total):
        full[pl.ds(pl.multiple_of(base_of(ug, 3), 8), ug), :] = total

    reduce_end(*gr, 2, put)

    def gather(stage, now):
        for o in range(1, radices[stage]):
            cp = gather_copy(full, send_a, recv_a, ug, stage, o, not now)
            if now:
                cp.start()
            else:
                cp.wait_recv()

    gather(2, True)
    reduce_end(*rr, 0)
    gather(2, False)
    gather(1, True)
    reduce_start(*rr, 1)
    gather(1, False)
    gather(0, True)
    reduce_end(*rr, 1)
    reduce_start(*rr, 2)
    gather(0, False)

    def put_share(total):
        share[...] = total

    reduce_end(*rr, 2, put_share)
    for stage in range(3):
        for o in range(1, radices[stage]):
            gather_copy(full, send_a, recv_a, ug, stage, o, False).wait_send()


def sums(sketch, panel, radices):
    rows, k = sketch.shape
    frames = panel.shape[1]
    ra, rb, rc = radices
    count = ra * rb * rc
    packed = len(pairs(k)) * BLK
    ug, ur = packed // count, frames // count
    parts = 4
    f32 = jnp.float32

    def slots(unit, width):
        return [
            pltpu.VMEM((ra, unit * rb * rc, width), f32),
            pltpu.VMEM((rb, unit * rc, width), f32),
            pltpu.VMEM((rc, unit, width), f32),
        ]

    most = max(radices)
    dma = pltpu.SemaphoreType.DMA
    return pl.pallas_call(
        functools.partial(sums_kernel, radices),
        out_shape=(jax.ShapeDtypeStruct((packed, BLK), f32), jax.ShapeDtypeStruct((ur, k), f32)),
        in_specs=[pl.BlockSpec(memory_space=pl.ANY)] * 2,
        out_specs=(pl.BlockSpec(memory_space=pltpu.VMEM),) * 2,
        scratch_shapes=[
            pltpu.VMEM((rows, k), f32), pltpu.VMEM((rows, frames), f32), pltpu.VMEM((k, 2 * k), f32),
            pltpu.VMEM((packed, BLK), f32), *slots(ug, BLK),
            pltpu.VMEM((frames, k), f32), *slots(ur, k),
            dma((2, parts)),
            dma((3, most)), dma((3, most)), dma((3, most)), dma((3, most)), dma((3, most)), dma((3, most)),
        ],
        compiler_params=pltpu.CompilerParams(
            collective_id=0, has_side_effects=True, vmem_limit_bytes=48 * 1024 * 1024),
    )(sketch, panel)


def basis_kernel(scale, g_ref, share_ref, s_ref, basis_ref, proj_ref, work, diag, dinv, wh, wl):
    n = work.shape[0]

    @pl.when(pl.program_id(0) == 0)
    def _():
        work[...] = jnp.zeros((n, n), jnp.float32)
        for i, (p, q) in enumerate(pairs(n)):
            work[p * BLK : (p + 1) * BLK, q * BLK : (q + 1) * BLK] = g_ref[i * BLK : (i + 1) * BLK, :]
        inverse_factor(work, diag, dinv)
        keep = lax.broadcasted_iota(jnp.int32, (n, n), 1) <= lax.broadcasted_iota(jnp.int32, (n, n), 0)
        w = jnp.where(keep, work[...], 0.0)
        hi, lo = split(w)
        wh[...] = hi
        wl[...] = lo
        proj_ref[...] = scale * lax.dot_general(
            share_ref[...], w, (((1,), (1,)), ((), ())), precision=HI, preferred_element_type=jnp.float32)

    def times(x, lo, hi, depth):
        nt = (((1,), (1,)), ((), ()))
        return lax.dot_general(x[:, :depth], lo[hi, :depth], nt, preferred_element_type=jnp.float32)

    sh, sl = split(s_ref[...])
    half = n // 2
    for at, depth in ((slice(0, half), half), (slice(half, n), n)):
        small = times(sh, wl, at, depth) + times(sl, wh, at, depth)
        basis_ref[:, at] = times(sh, wh, at, depth) + small


def finish(g, share, sketch, count):
    rows, k = sketch.shape
    tile = 256
    scale = 1.0 / (rows * count) ** 0.5
    f32 = jnp.float32
    return pl.pallas_call(
        functools.partial(basis_kernel, scale),
        grid=(rows // tile,),
        out_shape=(jax.ShapeDtypeStruct((rows, k), f32), jax.ShapeDtypeStruct(share.shape, f32)),
        in_specs=[
            pl.BlockSpec(g.shape, lambda i: (0, 0)),
            pl.BlockSpec(share.shape, lambda i: (0, 0)),
            pl.BlockSpec((tile, k), lambda i: (i, 0)),
        ],
        out_specs=(pl.BlockSpec((tile, k), lambda i: (i, 0)), pl.BlockSpec(share.shape, lambda i: (0, 0))),
        scratch_shapes=[
            pltpu.VMEM((k, k), f32), pltpu.VMEM((BLK, BLK), f32), pltpu.VMEM((BLK, BLK), f32),
            pltpu.VMEM((k, k), jnp.bfloat16), pltpu.VMEM((k, k), jnp.bfloat16),
        ],
        compiler_params=pltpu.CompilerParams(vmem_limit_bytes=32 * 1024 * 1024),
    )(g, share, sketch)


def plain_sums(sketch, panel):
    k = sketch.shape[1]
    total = sketch.shape[0] * lax.axis_size("rows")
    high = dict(precision=HI, preferred_element_type=jnp.float32)
    over = (((0,), (0,)), ((), ()))
    gram = lax.psum(lax.dot_general(sketch, sketch, over, **high) / total, "rows")
    share = lax.psum_scatter(lax.dot_general(panel, sketch, over, **high), "rows", scatter_dimension=0, tiled=True)
    blocks = [gram[p * BLK : (p + 1) * BLK, q * BLK : (q + 1) * BLK] for p, q in pairs(k)]
    return jnp.concatenate(blocks, axis=0), share


def on_device(sketch, panel):
    count = lax.axis_size("rows")
    k, frames = sketch.shape[1], panel.shape[1]
    packed = len(pairs(k)) * BLK
    if count % 8 == 0 and packed % (8 * count) == 0 and frames % (8 * count) == 0:
        g, share = sums(sketch, panel, (2, 4, count // 8))
    else:
        g, share = plain_sums(sketch, panel)
    return finish(g, share, sketch, count)


def solution(mesh):
    return jax.shard_map(
        on_device,
        mesh=mesh,
        in_specs=(P("rows", None), P("rows", None)),
        out_specs=(P("rows", None), P("rows", None)),
        check_vma=False,
    )
```

time: 330 us -> 69.5 us (0.21); the launches traced: 323 us -> 69.3 us
  other arithmetic: 123 us -> 0 us
  waiting for transfers between devices: 122 us -> 0 us
  Pallas kernels: 0 us -> 66.5 us
  matrix products: 45.5 us -> 0 us
  between operations: 17 us -> 0.65 us
  local copies, waits for them, and re-layouts: 15.4 us -> 2.18 us
    psum x1 -> x0, waiting for transfers between devices: 122 us -> none  [on_device(): gram = lax.psum(local_gram, 'rows')]
    another operation x17 -> x0, other arithmetic: 118 us -> none  [the longest x14 78.8 us: on_device(): lower = jnp.linalg.cholesky(gram)]
    pallas_call x0 -> x2, Pallas kernels: none -> 66.5 us  [the longest x1 36 us: sums(): pl.pallas_call(functools.partial(sums_kernel, radices), out_shape=(jax.Sh...]
    another operation x20 -> x0, matrix products: 23.9 us -> none  [the longest x7 17.8 us: on_device(): basis = jax.scipy.linalg.solve_triangular(lower, sketch.T, lower=True).T]
    dot_general x2 -> x0, matrix products: 21.6 us -> none  [the longest x1 11.2 us: on_device(): lax.dot_general(sketch, sketch, (((0,), (0,)), ((), ())), precision=highe...]
    another operation x17 -> x0, local copies, waits for them, and re-layouts: 8.54 us -> none
  transfers between devices with their start and end apart: 2 -> 0, of which waited for: 1 -> 0; matrix products, arithmetic and copies ran while one was open for 52% -> 0% of each run, Pallas kernels for 0% -> 0%
where the time goes in v1:
time: 69.5 us; the launch traced here: 69.3 us
  Pallas kernels  66.5 us (96%)
  local copies, waits for them, and re-layouts  2.18 us (3%)
    pallas_call x1, Pallas kernels, sums(): pl.pallas_call(functools.partial(sums_kernel, radices), out_shape=(jax.Sh...  36 us
    pallas_call x1, Pallas kernels, finish(): pl.pallas_call(functools.partial(basis_kernel, scale), grid=(rows // tile...  30.5 us
    unnamed x2, local copies, waits for them, and re-layouts  2.18 us

profile of v1, /device:TPU:0, one launch (start us, length us, event | category | flops | bytes accessed | tf_op | source)
XLA Modules:
  0.0 69.3 jit_solution(14387013890922683478)
XLA Ops:
  0.6 0.0 copy-start
  0.6 2.2 %copy-done = f32[2048,512]{1,0:T(8,128)S(1)} copy-done((f32[2048,512]{1,0:T(8,128)S(1)}, f32[2048,512]{1,0:T(8,128)}, u32[]{:S(2)}) %copy-start) | copy-done | bytes 4194328
  2.8 36.0 %shard_map.41 = (f32[1280,128]{1,0:T(8,128)S(1)}, f32[16,512]{1,0:T(8,128)S(1)}) custom-call(f32[2048,512]{1,0:T(8,128)S(1)} %copy-done, f32[2048,512]{1,0:T(8,128)} %p_hbm.1), custom_call_target="tpu_custom_call" | custom-call | tf_op jit(solution)/shard_map/pallas_call | solution.py:320
  38.8 30.5 %shard_map.42 = (f32[2048,512]{1,0:T(8,128)}, f32[16,512]{1,0:T(8,128)}) custom-call(f32[1280,128]{1,0:T(8,128)S(1)} %get-tuple-element.4.g_ref, f32[16,512]{1,0:T(8,128)S(1)} %get-tuple-element.5.share_ref, f32[2048,512]{1,0:T(8,128)S(1)} %copy-done), custom_call_target="tpu_custom_call" | custom-call | tf_op jit(solution)/shard_map/pallas_call | solution.py:370
Async XLA Ops:
  0.6 2.2 %copy-start = (f32[2048,512]{1,0:T(8,128)S(1)}, f32[2048,512]{1,0:T(8,128)}, u32[]{:S(2)}) copy-start(f32[2048,512]{1,0:T(8,128)} %s_ref.1) | copy-start | bytes 12582916

commit v2 on v1

--- a/solution.py
+++ b/solution.py
@@ -9,10 +9,7 @@
 HI = lax.Precision.HIGHEST
 BLK = 128
 SUB = 8
-
-
-def splat(x, i, j):
-    return jnp.broadcast_to(x[i : i + 1, j : j + 1], (SUB, BLK))
+GROUP = 64
 
 
 def row(x, i):
@@ -43,46 +40,68 @@
     return t
 
 
-def block_inverse(a_ref, out_ref, base):
+def block_inverse(a_ref, out_ref):
     lanes = lax.broadcasted_iota(jnp.int32, (SUB, BLK), 1)
     subs = lax.broadcasted_iota(jnp.int32, (SUB, BLK), 0)
-    steps = BLK // SUB
-    strips = [a_ref[i * SUB : (i + 1) * SUB, :] for i in range(steps)]
-    for j in range(steps):
-        j0 = j * SUB
-        cur = strips[j]
-        cols = [lane(cur, j0 + m) for m in range(SUB)]
-        a = [[row(cols[m], i) for m in range(i + 1)] for i in range(SUB)]
-        t = small_inverse(a)
-        here = (lanes >= j0) & (lanes < j0 + SUB)
-        mixed = jnp.where(here, jnp.where(lanes - j0 == subs, 1.0, 0.0), cur)
-        rows = [row(mixed, m) for m in range(SUB)]
-        r = []
-        for k in range(SUB):
-            acc = t[k][0] * rows[0]
-            for m in range(1, k + 1):
-                acc = acc + t[k][m] * rows[m]
-            r.append(acc)
-        if j + 1 < steps:
-            q = []
+    per = GROUP // SUB
+    rest = a_ref[...]
+    for g0 in range(0, BLK, GROUP):
+        strips = [rest[i * SUB : (i + 1) * SUB, :] for i in range(per)]
+        later = rest[GROUP:, :]
+        done = []
+        x = [row(strips[0], i) for i in range(SUB)]
+        for j in range(per):
+            j0 = g0 + j * SUB
+            t = small_inverse([[lane(x[i], j0 + m) for m in range(i + 1)] for i in range(SUB)])
+            here = (lanes >= j0) & (lanes < j0 + SUB)
+            rows = [jnp.where(here, jnp.where(lanes == j0 + m, 1.0, 0.0), x[m]) for m in range(SUB)]
+            near = j + 1 < per
+            if near:
+                c = [[lane(x[k], j0 + SUB + i) for k in range(SUB)] for i in range(SUB)]
+                ahead = [jnp.where(here, 0.0, row(strips[j + 1], i)) for i in range(SUB)]
+            r = []
             for k in range(SUB):
-                acc = t[k][k] * r[k]
-                for m in range(k + 1, SUB):
-                    acc = acc + t[m][k] * r[m]
-                q.append(acc)
-            for i in range(j + 1, steps):
-                x = strips[i]
-                new = jnp.where(here, 0.0, x)
-                for m in range(SUB):
-                    new = new - lane(x, j0 + m) * q[m]
-                strips[i] = new
-        res = r[0]
-        for k in range(1, SUB):
-            res = jnp.where(subs == k, r[k], res)
-        out_ref[j0 : j0 + SUB, :] = jnp.where(lanes <= j0 + subs, res, 0.0)
-
-
-def inverse_factor(work, diag, dinv):
+                acc = t[k][0] * rows[0]
+                for m in range(1, k + 1):
+                    acc = acc + t[k][m] * rows[m]
+                r.append(acc)
+            if near:
+                q = []
+                for k in range(SUB):
+                    acc = t[SUB - 1][k] * r[SUB - 1]
+                    for m in range(SUB - 2, k - 1, -1):
+                        acc = acc + t[m][k] * r[m]
+                    q.append(acc)
+                x = []
+                for i in range(SUB):
+                    s0 = c[i][0] * q[0]
+                    s1 = c[i][1] * q[1]
+                    for m in range(2, SUB, 2):
+                        s0 = s0 + c[i][m] * q[m]
+                        s1 = s1 + c[i][m + 1] * q[m + 1]
+                    x.append(ahead[i] - (s0 + s1))
+                for i in range(j + 2, per):
+                    old = strips[i]
+                    strip = jnp.where(here, 0.0, old)
+                    for m in range(SUB):
+                        strip = strip - lane(old, j0 + m) * q[m]
+                    strips[i] = strip
+            res = r[0]
+            for k in range(1, SUB):
+                res = jnp.where(subs == k, r[k], res)
+            done.append(res)
+            out_ref[j0 : j0 + SUB, :] = jnp.where(lanes <= j0 + subs, res, 0.0)
+        if g0 + GROUP < BLK:
+            u = jnp.concatenate(done, axis=0)
+            wide = lax.broadcasted_iota(jnp.int32, later.shape, 1)
+            kept = jnp.where((wide >= g0) & (wide < g0 + GROUP), 0.0, later)
+            own = lax.broadcasted_iota(jnp.int32, u.shape, 1) - g0
+            dead = (own < GROUP) & (own > lax.broadcasted_iota(jnp.int32, u.shape, 0))
+            full = lax.dot_general(u, jnp.where(dead, 0.0, u), (((0,), (0,)), ((), ())), precision=HI, preferred_element_type=jnp.float32)
+            rest = kept - full[g0 + GROUP :, :]
+
+
+def inverse_factor(work, diag, dinv, between=lambda p: None):
     n = work.shape[0]
     blocks = n // BLK
     ids = lax.broadcasted_iota(jnp.int32, (BLK, n), 1)
@@ -91,7 +110,7 @@
     def outer(p, c):
         at = pl.multiple_of(p * BLK, BLK)
         diag[...] = work[pl.ds(at, BLK), pl.ds(at, BLK)]
-        block_inverse(diag, dinv, 0)
+        block_inverse(diag, dinv)
         work[pl.ds(at, BLK), pl.ds(at, BLK)] = jnp.where(
             lax.broadcasted_iota(jnp.int32, (BLK, BLK), 0) == lax.broadcasted_iota(jnp.int32, (BLK, BLK), 1), 1.0, 0.0)
         r = jnp.dot(dinv[...], work[pl.ds(at, BLK), :], precision=HI, preferred_element_type=jnp.float32)
@@ -105,6 +124,7 @@
             return c
 
         lax.fori_loop(p + 1, blocks, update, 0)
+        between(p)
         return c
 
     lax.fori_loop(0, blocks, outer, 0)
@@ -125,8 +145,8 @@
 
 
 def sums_kernel(
-    radices, s_hbm, p_hbm, full, share,
-    s_buf, p_buf, gacc, g, g1, g2, g3, r, r1, r2, r3, in_sem,
+    radices, s_hbm, p_hbm, inverse, share,
+    work, diag, dinv, full, s_buf, p_buf, gacc, g, g1, g2, g3, r, r1, r2, r3, in_sem,
     send_g, recv_g, send_r, recv_r, send_a, recv_a,
 ):
     ra, rb, rc = radices
@@ -263,7 +283,6 @@
     reduce_end(*gr, 1)
     reduce_start(*gr, 2)
     rr = (r, (r1, r2, r3), send_r, recv_r, fr)
-    reduce_start(*rr, 0)
 
     def put(total):
         full[pl.ds(pl.multiple_of(base_of(ug, 3), 8), ug), :] = total
@@ -278,21 +297,33 @@
             else:
                 cp.wait_recv()
 
-    gather(2, True)
-    reduce_end(*rr, 0)
-    gather(2, False)
-    gather(1, True)
-    reduce_start(*rr, 1)
-    gather(1, False)
-    gather(0, True)
-    reduce_end(*rr, 1)
-    reduce_start(*rr, 2)
-    gather(0, False)
+    for stage in (2, 1, 0):
+        gather(stage, True)
+        gather(stage, False)
+
+    reduce_start(*rr, 0)
+    work[...] = jnp.zeros((k, k), jnp.float32)
+    for i, (p, q) in enumerate(pairs(k)):
+        work[p * BLK : (p + 1) * BLK, q * BLK : (q + 1) * BLK] = full[i * BLK : (i + 1) * BLK, :]
 
     def put_share(total):
         share[...] = total
 
+    def between(p):
+        @pl.when(p == 0)
+        def _():
+            reduce_end(*rr, 0)
+            reduce_start(*rr, 1)
+
+        @pl.when(p == 1)
+        def _():
+            reduce_end(*rr, 1)
+            reduce_start(*rr, 2)
+
+    inverse_factor(work, diag, dinv, between)
     reduce_end(*rr, 2, put_share)
+    keep = lax.broadcasted_iota(jnp.int32, (k, k), 1) <= lax.broadcasted_iota(jnp.int32, (k, k), 0)
+    inverse[...] = jnp.where(keep, work[...], 0.0)
     for stage in range(3):
         for o in range(1, radices[stage]):
             gather_copy(full, send_a, recv_a, ug, stage, o, False).wait_send()
@@ -319,10 +350,12 @@
     dma = pltpu.SemaphoreType.DMA
     return pl.pallas_call(
         functools.partial(sums_kernel, radices),
-        out_shape=(jax.ShapeDtypeStruct((packed, BLK), f32), jax.ShapeDtypeStruct((ur, k), f32)),
+        out_shape=(jax.ShapeDtypeStruct((k, k), f32), jax.ShapeDtypeStruct((ur, k), f32)),
         in_specs=[pl.BlockSpec(memory_space=pl.ANY)] * 2,
         out_specs=(pl.BlockSpec(memory_space=pltpu.VMEM),) * 2,
         scratch_shapes=[
+            pltpu.VMEM((k, k), f32), pltpu.VMEM((BLK, BLK), f32), pltpu.VMEM((BLK, BLK), f32),
+            pltpu.VMEM((packed, BLK), f32),
             pltpu.VMEM((rows, k), f32), pltpu.VMEM((rows, frames), f32), pltpu.VMEM((k, 2 * k), f32),
             pltpu.VMEM((packed, BLK), f32), *slots(ug, BLK),
             pltpu.VMEM((frames, k), f32), *slots(ur, k),
@@ -330,21 +363,36 @@
             dma((3, most)), dma((3, most)), dma((3, most)), dma((3, most)), dma((3, most)), dma((3, most)),
         ],
         compiler_params=pltpu.CompilerParams(
-            collective_id=0, has_side_effects=True, vmem_limit_bytes=48 * 1024 * 1024),
+            collective_id=0, has_side_effects=True, vmem_limit_bytes=60 * 1024 * 1024),
     )(sketch, panel)
 
 
-def basis_kernel(scale, g_ref, share_ref, s_ref, basis_ref, proj_ref, work, diag, dinv, wh, wl):
-    n = work.shape[0]
+def factor_kernel(g_ref, inverse, work, diag, dinv):
+    k = work.shape[0]
+    work[...] = jnp.zeros((k, k), jnp.float32)
+    for i, (p, q) in enumerate(pairs(k)):
+        work[p * BLK : (p + 1) * BLK, q * BLK : (q + 1) * BLK] = g_ref[i * BLK : (i + 1) * BLK, :]
+    inverse_factor(work, diag, dinv)
+    keep = lax.broadcasted_iota(jnp.int32, (k, k), 1) <= lax.broadcasted_iota(jnp.int32, (k, k), 0)
+    inverse[...] = jnp.where(keep, work[...], 0.0)
+
+
+def factor(g, k):
+    f32 = jnp.float32
+    return pl.pallas_call(
+        factor_kernel,
+        out_shape=jax.ShapeDtypeStruct((k, k), f32),
+        scratch_shapes=[pltpu.VMEM((k, k), f32), pltpu.VMEM((BLK, BLK), f32), pltpu.VMEM((BLK, BLK), f32)],
+        compiler_params=pltpu.CompilerParams(vmem_limit_bytes=32 * 1024 * 1024),
+    )(g)
+
+
+def basis_kernel(scale, w_ref, share_ref, s_ref, basis_ref, proj_ref, wh, wl):
+    n = w_ref.shape[0]
 
     @pl.when(pl.program_id(0) == 0)
     def _():
-        work[...] = jnp.zeros((n, n), jnp.float32)
-        for i, (p, q) in enumerate(pairs(n)):
-            work[p * BLK : (p + 1) * BLK, q * BLK : (q + 1) * BLK] = g_ref[i * BLK : (i + 1) * BLK, :]
-        inverse_factor(work, diag, dinv)
-        keep = lax.broadcasted_iota(jnp.int32, (n, n), 1) <= lax.broadcasted_iota(jnp.int32, (n, n), 0)
-        w = jnp.where(keep, work[...], 0.0)
+        w = w_ref[...]
         hi, lo = split(w)
         wh[...] = hi
         wl[...] = lo
@@ -362,7 +410,7 @@
         basis_ref[:, at] = times(sh, wh, at, depth) + small
 
 
-def finish(g, share, sketch, count):
+def finish(w, share, sketch, count):
     rows, k = sketch.shape
     tile = 256
     scale = 1.0 / (rows * count) ** 0.5
@@ -372,17 +420,16 @@
         grid=(rows // tile,),
         out_shape=(jax.ShapeDtypeStruct((rows, k), f32), jax.ShapeDtypeStruct(share.shape, f32)),
         in_specs=[
-            pl.BlockSpec(g.shape, lambda i: (0, 0)),
+            pl.BlockSpec(w.shape, lambda i: (0, 0)),
             pl.BlockSpec(share.shape, lambda i: (0, 0)),
             pl.BlockSpec((tile, k), lambda i: (i, 0)),
         ],
         out_specs=(pl.BlockSpec((tile, k), lambda i: (i, 0)), pl.BlockSpec(share.shape, lambda i: (0, 0))),
         scratch_shapes=[
-            pltpu.VMEM((k, k), f32), pltpu.VMEM((BLK, BLK), f32), pltpu.VMEM((BLK, BLK), f32),
             pltpu.VMEM((k, k), jnp.bfloat16), pltpu.VMEM((k, k), jnp.bfloat16),
         ],
-        compiler_params=pltpu.CompilerParams(vmem_limit_bytes=32 * 1024 * 1024),
-    )(g, share, sketch)
+        compiler_params=pltpu.CompilerParams(vmem_limit_bytes=60 * 1024 * 1024),
+    )(w, share, sketch)
 
 
 def plain_sums(sketch, panel):
@@ -401,10 +448,11 @@
     k, frames = sketch.shape[1], panel.shape[1]
     packed = len(pairs(k)) * BLK
     if count % 8 == 0 and packed % (8 * count) == 0 and frames % (8 * count) == 0:
-        g, share = sums(sketch, panel, (2, 4, count // 8))
+        w, share = sums(sketch, panel, (2, 4, count // 8))
     else:
         g, share = plain_sums(sketch, panel)
-    return finish(g, share, sketch, count)
+        w = factor(g, k)
+    return finish(w, share, sketch, count)
 
 
 def solution(mesh):

time: 69.5 us -> 60.1 us (0.86)
  Pallas kernels: 66.5 us -> 58.9 us
  local copies, waits for them, and re-layouts: 2.18 us -> 0 us
    pallas_call x1, Pallas kernels: 30.5 us -> 9.65 us  [finish(): pl.pallas_call(functools.partial(basis_kernel, scale), grid=(rows // tile...]
    pallas_call x1, Pallas kernels: 36 us -> 49.3 us  [sums(): pl.pallas_call(functools.partial(sums_kernel, radices), out_shape=(jax.Sh...]
    unnamed x2 -> x0, local copies, waits for them, and re-layouts: 2.18 us -> none
where the time goes in v2:
time: 60.1 us; the launch traced here: 59.5 us
  Pallas kernels  58.9 us (98%)
  between operations  0.64 us (1%)
    pallas_call x1, Pallas kernels, sums(): pl.pallas_call(functools.partial(sums_kernel, radices), out_shape=(jax.Sh...  49.3 us
    pallas_call x1, Pallas kernels, finish(): pl.pallas_call(functools.partial(basis_kernel, scale), grid=(rows // tile...  9.65 us

profile of v2, /device:TPU:0, one launch (start us, length us, event | category | flops | bytes accessed | tf_op | source)
XLA Modules:
  0.0 59.5 jit_solution(16332858805001729463)
XLA Ops:
  0.6 49.3 %shard_map.41 = (f32[512,512]{1,0:T(8,128)}, f32[16,512]{1,0:T(8,128)}) custom-call(f32[2048,512]{1,0:T(8,128)} %s_ref.1, f32[2048,512]{1,0:T(8,128)} %p_hbm.1), custom_call_target="tpu_custom_call" | custom-call | tf_op jit(solution)/shard_map/pallas_call | solution.py:351
  49.9 9.7 %shard_map.42 = (f32[2048,512]{1,0:T(8,128)}, f32[16,512]{1,0:T(8,128)}) custom-call(f32[512,512]{1,0:T(8,128)} %get-tuple-element.4.w_ref, f32[16,512]{1,0:T(8,128)} %get-tuple-element.5.share_ref, f32[2048,512]{1,0:T(8,128)} %s_ref.1), custom_call_target="tpu_custom_call" | custom-call | tf_op jit(solution)/shard_map/pallas_call | solution.py:418

commit v3 on v2

--- a/solution.py
+++ b/solution.py
@@ -447,8 +447,8 @@
     count = lax.axis_size("rows")
     k, frames = sketch.shape[1], panel.shape[1]
     packed = len(pairs(k)) * BLK
-    if count % 8 == 0 and packed % (8 * count) == 0 and frames % (8 * count) == 0:
-        w, share = sums(sketch, panel, (2, 4, count // 8))
+    if count % 16 == 0 and packed % (8 * count) == 0 and frames % (8 * count) == 0:
+        w, share = sums(sketch, panel, (2, 8, count // 16))
     else:
         g, share = plain_sums(sketch, panel)
         w = factor(g, k)

time: 60.1 us -> 59.4 us (0.988)
  no operation moved by 1% of the time
where the time goes in v3:
time: 59.4 us; the launch traced here: 59.1 us
  Pallas kernels  58.5 us (98%)
  between operations  0.64 us (1%)
    pallas_call x1, Pallas kernels, sums(): pl.pallas_call(functools.partial(sums_kernel, radices), out_shape=(jax.Sh...  48.8 us
    pallas_call x1, Pallas kernels, finish(): pl.pallas_call(functools.partial(basis_kernel, scale), grid=(rows // tile...  9.65 us

profile of v3, /device:TPU:0, one launch (start us, length us, event | category | flops | bytes accessed | tf_op | source)
XLA Modules:
  0.0 59.1 jit_solution(3424524316113131411)
XLA Ops:
  0.6 48.8 %shard_map.41 = (f32[512,512]{1,0:T(8,128)}, f32[16,512]{1,0:T(8,128)}) custom-call(f32[2048,512]{1,0:T(8,128)} %s_ref.1, f32[2048,512]{1,0:T(8,128)} %p_hbm.1), custom_call_target="tpu_custom_call" | custom-call | tf_op jit(solution)/shard_map/pallas_call | solution.py:351
  49.5 9.7 %shard_map.42 = (f32[2048,512]{1,0:T(8,128)}, f32[16,512]{1,0:T(8,128)}) custom-call(f32[512,512]{1,0:T(8,128)} %get-tuple-element.4.w_ref, f32[16,512]{1,0:T(8,128)} %get-tuple-element.5.share_ref, f32[2048,512]{1,0:T(8,128)} %s_ref.1), custom_call_target="tpu_custom_call" | custom-call | tf_op jit(solution)/shard_map/pallas_call | solution.py:418
